TPU v7x, 128 devices: a whole 4x4x4 slice. The times are simulated.
128 devices in a mesh: dp: 16 (over x, z_hi, core), sub: 8 (over z_lo, y).
Axes of the slice: x: 4, y: 4, z: 4 (z_hi: 2, z_lo: 2; z = z_hi * 2 + z_lo), core: 2. Of those that a mesh axis runs over, the one named last changes fastest.
Arguments:
- embeddings: bfloat16 [131072, 1024], P(('dp', 'sub')), may hold values from -4 to 4
- partner: int32 [131072], P(('dp', 'sub')), may hold values from 0 to 131071, as said below
- prior_lse: float32 [131072], P(('dp', 'sub')), may hold values from 4 to 11
Outputs:
- gradient: float32 [131072, 1024], P(('dp', 'sub'))
- row_lse: float32 [131072], P(('dp', 'sub'))
Inputs may be any that keep to these rules, and one draw needn't show every extreme that they name: partner[i] lies in the same aligned block of 1024 rows as i and differs from i.
All inputs are finite; a program needn't handle non-finite values.
Results may differ from a plain program's by a relative error of at most 0.0015.
Values may be sent and summed in bfloat16 or wider, within the bound.
A program may use at most 64 MiB of HBM per device.

v0:
```python
from functools import reduce

import jax
import jax.numpy as jnp
from jax import lax
from jax.sharding import PartitionSpec as P

FIRST_STEP = 1


SCALE = 20.0


def passed_along(block, axis, distance):
    devices = range(lax.axis_size(axis))
    route = [((i - distance) % len(devices), i) for i in devices]
    return lax.ppermute(block, axis, route)


def similarity(left, right):
    return SCALE * lax.dot_general(
        left, right, (((1,), (1,)), ((), ())), preferred_element_type=jnp.float32
    )


def masked_self(block):
    scores = similarity(block, block)
    count = scores.shape[0]
    diagonal = lax.broadcasted_iota(jnp.int32, (count, count), 0) == lax.broadcasted_iota(
        jnp.int32, (count, count), 1
    )
    return jnp.where(diagonal, -jnp.inf, scores)


def row_extrema(scores):
    peak = jnp.max(scores, axis=1)
    total = jnp.sum(jnp.exp(scores - peak[:, None]), axis=1)
    return (peak, total)


def column_extrema(scores):
    peak = jnp.max(scores, axis=0)
    total = jnp.sum(jnp.exp(scores - peak[None, :]), axis=0)
    return (peak, total)


def merge_stats(pairs):
    peak = reduce(jnp.maximum, [entry[0] for entry in pairs])
    total = reduce(jnp.add, [entry[1] * jnp.exp(entry[0] - peak) for entry in pairs])
    return peak + jnp.log(total)


def self_weights(own_tile, lse_rows, local_pos):
    count = own_tile.shape[0]
    onehot = (local_pos[:, None] == lax.broadcasted_iota(jnp.int32, (count, count), 1)).astype(
        jnp.float32
    )
    chances = jnp.exp(own_tile - lse_rows[:, None]) - onehot
    return (chances + chances.T).astype(jnp.bfloat16)


def pair_weights(scores, lse_rows, other_lse):
    return (jnp.exp(scores - lse_rows[:, None]) + jnp.exp(scores - other_lse[None, :])).astype(
        jnp.bfloat16
    )


def transposed_product(weights, block):
    return lax.dot_general(
        weights, block, (((0,), (0,)), ((), ())), preferred_element_type=jnp.float32
    )


def per_device(embeddings, partner, prior_lse):
    row_count = embeddings.shape[0]
    first_step = FIRST_STEP
    second_step = lax.axis_size("sub") + 1
    local_pos = partner % row_count
    own_tile = masked_self(embeddings)
    prior_pair = (prior_lse, jnp.ones_like(prior_lse))
    from_first = passed_along(embeddings, ("dp", "sub"), -first_step)
    from_second = passed_along(embeddings, ("dp", "sub"), -second_step)
    first_scores = similarity(embeddings, from_first)
    second_scores = similarity(embeddings, from_second)
    peak_first, total_first = column_extrema(first_scores)
    back_first = passed_along((peak_first, total_first), ("dp", "sub"), first_step)
    peak_second, total_second = column_extrema(second_scores)
    back_second = passed_along((peak_second, total_second), ("dp", "sub"), second_step)
    row_lse = merge_stats(
        [
            row_extrema(own_tile),
            prior_pair,
            row_extrema(first_scores),
            row_extrema(second_scores),
            back_first,
            back_second,
        ]
    )
    lse_first = passed_along(row_lse, ("dp", "sub"), -first_step)
    lse_second = passed_along(row_lse, ("dp", "sub"), -second_step)
    weights_first = pair_weights(first_scores, row_lse, lse_first)
    weights_second = pair_weights(second_scores, row_lse, lse_second)
    partial_first = transposed_product(weights_first, embeddings).astype(jnp.bfloat16)
    partial_second = transposed_product(weights_second, embeddings).astype(jnp.bfloat16)
    gradient = jnp.dot(
        self_weights(own_tile, row_lse, local_pos), embeddings, preferred_element_type=jnp.float32
    )
    gradient = gradient + jnp.dot(weights_first, from_first, preferred_element_type=jnp.float32)
    gradient = gradient + jnp.dot(weights_second, from_second, preferred_element_type=jnp.float32)
    gradient = gradient + passed_along(partial_first, ("dp", "sub"), first_step).astype(jnp.float32)
    gradient = gradient + passed_along(partial_second, ("dp", "sub"), second_step).astype(
        jnp.float32
    )
    return (SCALE * gradient, row_lse)


def solution(mesh):
    placed = (P(("dp", "sub"), None), P(("dp", "sub")), P(("dp", "sub")))
    return jax.shard_map(
        per_device,
        mesh=mesh,
        in_specs=placed,
        out_specs=(P(("dp", "sub"), None), P(("dp", "sub"))),
        check_vma=False,
    )
```

profile of v0, /device:TPU:1, one launch (start us, length us, event | category | flops | bytes accessed | tf_op | source)
XLA Modules:
  0.0 223.5 jit_solution(1140752540704872058)
XLA Ops:
  0.6 5.6 %collective-permute-start = (bf16[1024,1024]{1,0:T(8,128)(2,1)}, bf16[1024,1024]{1,0:T(8,128)(2,1)S(1)}, u32[]{:S(2)}, u32[]{:S(2)}) collective-permute-start(bf16[1024,1024]{1,0:T(8,128)(2,1)} %param.3), channel_id=1, source_target_pairs={{1,0},{2,1},{3,2},{4,3},{5,4},{6,5},{7,6},{8,7},{9,8},{10,9},{11,1... | collective-permute-start | bytes 6291464 | tf_op jit(solution)/shard_map/ppermute | solution.py:17
  6.2 4.2 %collective-permute-start.1 = (bf16[1024,1024]{1,0:T(8,128)(2,1)}, bf16[1024,1024]{1,0:T(8,128)(2,1)}, u32[]{:S(2)}, u32[]{:S(2)}) collective-permute-start(bf16[1024,1024]{1,0:T(8,128)(2,1)} %param.3), channel_id=1, source_target_pairs={{9,0},{10,1},{11,2},{12,3},{13,4},{14,5},{15,6},{16,7},{17,8},{18,... | collective-permute-start | bytes 6291464 | tf_op jit(solution)/shard_map/ppermute | solution.py:17
  10.4 6.6 %convolution_multiply_fusion = f32[1024,1024]{0,1:T(8,128)} fusion(bf16[1024,1024]{1,0:T(8,128)(2,1)} %param.3), kind=kOutput, calls=%fused_computation.24 | convolution fusion | flops 2148532224 | bytes 6291456 | tf_op jit(solution)/shard_map/dot_general | solution.py:21
  17.0 5.3 %copy.6 = f32[1024,1024]{1,0:T(8,128)} copy(f32[1024,1024]{0,1:T(8,128)} %convolution_multiply_fusion) | data formatting | bytes 8388608 | tf_op jit(solution)/shard_map/mul | solution.py:21
  22.4 2.6 %fusion.6 = f32[1024]{0:T(1024)S(1)} fusion(f32[1024,1024]{1,0:T(8,128)} %copy.6), kind=kLoop, calls=%fused_computation.19 | loop fusion | flops 3144704 | bytes 4198400 | tf_op jit(solution)/shard_map/reduce_max | solution.py:36
  25.0 71.9 %collective-permute-done = bf16[1024,1024]{1,0:T(8,128)(2,1)S(1)} collective-permute-done((bf16[1024,1024]{1,0:T(8,128)(2,1)}, bf16[1024,1024]{1,0:T(8,128)(2,1)S(1)}, u32[]{:S(2)}, u32[]{:S(2)}) %collective-permute-start) | collective-permute-done | bytes 2097184 | tf_op jit(solution)/shard_map/ppermute | solution.py:17
  96.9 0.0 copy-done.5
  96.9 2.5 %multiply_reduce_fusion.3 = (f32[1024]{0:T(1024)S(1)}, f32[1024,1024]{1,0:T(8,128)S(1)}) fusion(bf16[1024,1024]{1,0:T(8,128)(2,1)S(1)} %copy-done.5, bf16[1024,1024]{1,0:T(8,128)(2,1)S(1)} %collective-permute-done), kind=kOutput, calls=%fused_computation.23 | convolution fusion | flops 2149579776 | bytes 8392704 | tf_op jit(solution)/shard_map/dot_general | solution.py:21
  99.4 0.0 copy-done.6
  99.4 1.1 exponential_reduce_fusion.3
  100.6 0.1 collective-permute-start.2
  100.7 0.7 exponential_reduce_fusion.1
  101.4 0.0 collective-permute-done.1
  101.4 4.1 %multiply_reduce_fusion.1 = (f32[1024]{0:T(1024)S(1)}, f32[1024,1024]{1,0:T(8,128)S(1)}) fusion(bf16[1024,1024]{1,0:T(8,128)(2,1)S(1)} %copy-done.5, bf16[1024,1024]{1,0:T(8,128)(2,1)} %collective-permute-done.1), kind=kOutput, calls=%fused_computation.21 | convolution fusion | flops 2149579776 | bytes 8392704 | tf_op jit(solution)/shard_map/dot_general | solution.py:21
  105.5 1.1 exponential_reduce_fusion.2
  106.6 0.0 copy-start.2
  106.7 0.0 copy-start.4
  106.7 0.7 exponential_reduce_fusion
  107.4 0.3 collective-permute-start.3
  107.7 0.1 collective-permute-start.4
  107.8 0.1 collective-permute-start.5
  107.8 0.0 copy-done
  107.9 0.9 exponential_reduce_fusion.4
  108.8 4.7 %collective-permute-done.4 = f32[1024]{0:T(1024)S(1)} collective-permute-done((f32[1024]{0:T(1024)S(1)}, f32[1024]{0:T(1024)S(1)}, u32[]{:S(2)}, u32[]{:S(2)}) %collective-permute-start.4) | collective-permute-done | bytes 4128 | tf_op jit(solution)/shard_map/ppermute | solution.py:17
  113.5 0.0 collective-permute-done.2
  113.5 2.4 %collective-permute-done.5 = f32[1024]{0:T(1024)S(1)} collective-permute-done((f32[1024]{0:T(1024)S(1)}, f32[1024]{0:T(1024)S(1)}, u32[]{:S(2)}, u32[]{:S(2)}) %collective-permute-start.5) | collective-permute-done | bytes 4128 | tf_op jit(solution)/shard_map/ppermute | solution.py:17
  115.9 0.0 collective-permute-done.3
  115.9 0.0 copy-done.2
  115.9 0.0 copy-start.3
  115.9 3.0 %collective-permute-start.7 = (f32[1024]{0:T(1024)S(1)}, f32[1024]{0:T(1024)S(1)}, u32[]{:S(2)}, u32[]{:S(2)}) collective-permute-start(f32[1024]{0:T(1024)S(1)} %log_add_fusion), channel_id=1, source_target_pairs={{9,0},{10,1},{11,2},{12,3},{13,4},{14,5},{15,6},{16,7},{17,8},{18,... | collective-permute-start | bytes 12296 | tf_op jit(solution)/shard_map/ppermute | solution.py:17
  119.0 0.0 copy-done.4
  119.0 2.7 %collective-permute-start.6 = (f32[1024]{0:T(1024)S(1)}, f32[1024]{0:T(1024)S(1)}, u32[]{:S(2)}, u32[]{:S(2)}) collective-permute-start(f32[1024]{0:T(1024)S(1)} %log_add_fusion), channel_id=1, source_target_pairs={{1,0},{2,1},{3,2},{4,3},{5,4},{6,5},{7,6},{8,7},{9,8},{10,9},{11,1... | collective-permute-start | bytes 12296 | tf_op jit(solution)/shard_map/ppermute | solution.py:17
  121.7 0.0 collective-permute-done.7
  121.7 2.9 %convolution_convert_fusion = bf16[1024,1024]{1,0:T(8,128)(2,1)S(1)} fusion(bf16[1024,1024]{1,0:T(8,128)(2,1)S(1)} %copy-done.5, f32[1024,1024]{1,0:T(8,128)S(1)} %get-tuple-element.7, f32[1024]{0:T(1024)S(1)} %collective-permute-done.7, f32[1024]{0:T(1024)S(1)} %log_add_fusion), kind=kOutput, calls=%fused_computation.26 | convolution fusion | flops 2153775104 | bytes 8396800 | tf_op jit(solution)/shard_map/dot_general | solution.py:69
  124.6 0.0 copy-start.1
  124.6 2.0 collective-permute-start.9
  126.6 0.0 collective-permute-done.6
  126.6 2.9 %convolution_convert_fusion.1 = bf16[1024,1024]{1,0:T(8,128)(2,1)S(1)} fusion(bf16[1024,1024]{1,0:T(8,128)(2,1)S(1)} %copy-done.5, f32[1024,1024]{1,0:T(8,128)S(1)} %get-tuple-element.9, f32[1024]{0:T(1024)S(1)} %collective-permute-done.6, f32[1024]{0:T(1024)S(1)} %log_add_fusion), kind=kOutput, calls=%fused_computation.27 | convolution fusion | flops 2153775104 | bytes 8396800 | tf_op jit(solution)/shard_map/dot_general | solution.py:69
  129.5 0.0 copy-start.7
  129.6 0.3 collective-permute-start.8
  129.9 3.5 %fusion.7 = f32[1024,1024]{1,0:T(8,128)S(1)} fusion(bf16[1024,1024]{1,0:T(8,128)(2,1)S(1)} %copy-done.5, f32[1024,1024]{0,1:T(8,128)S(1)} %copy-done.1, f32[1024,1024]{1,0:T(8,128)S(1)} %copy-done, s32[1024]{0:T(1024)S(1)} %add_select_fusion, f32[1024]{0:T(1024)S(1)} %log_add_fusion), kind=kOutput, calls=%fused_computation.25 | convolution fusion | flops 2162163712 | bytes 14688256 | tf_op jit(solution)/shard_map/dot_general | solution.py:105
  133.4 0.0 copy-done.7
  133.4 2.8 %fusion.11 = f32[1024,1024]{1,0:T(8,128)S(1)} fusion(bf16[1024,1024]{1,0:T(8,128)(2,1)S(1)} %copy-done.7, f32[1024,1024]{1,0:T(8,128)S(1)} %get-tuple-element.9, f32[1024]{0:T(1024)S(1)} %collective-permute-done.6, f32[1024]{0:T(1024)S(1)} %log_add_fusion), kind=kOutput, calls=%fused_computation.34 | convolution fusion | flops 2152726528 | bytes 10493952 | tf_op jit(solution)/shard_map/dot_general | solution.py:108
  136.2 0.0 copy-done.3
  136.2 4.4 %fusion.12 = f32[1024,1024]{1,0:T(8,128)S(1)} fusion(bf16[1024,1024]{1,0:T(8,128)(2,1)} %collective-permute-done.1, f32[1024,1024]{1,0:T(8,128)S(1)} %get-tuple-element.7, f32[1024]{0:T(1024)S(1)} %collective-permute-done.7, f32[1024]{0:T(1024)S(1)} %log_add_fusion), kind=kOutput, calls=%fused_computation.35 | convolution fusion | flops 2152726528 | bytes 10493952 | tf_op jit(solution)/shard_map/dot_general | solution.py:109
  140.6 35.3 %collective-permute-done.9 = bf16[1024,1024]{1,0:T(8,128)(2,1)} collective-permute-done((bf16[1024,1024]{1,0:T(8,128)(2,1)S(1)}, bf16[1024,1024]{1,0:T(8,128)(2,1)}, u32[]{:S(2)}, u32[]{:S(2)}) %collective-permute-start.9) | collective-permute-done | bytes 2097184 | tf_op jit(solution)/shard_map/ppermute | solution.py:17
  175.9 41.5 %collective-permute-done.8 = bf16[1024,1024]{1,0:T(8,128)(2,1)} collective-permute-done((bf16[1024,1024]{1,0:T(8,128)(2,1)S(1)}, bf16[1024,1024]{1,0:T(8,128)(2,1)}, u32[]{:S(2)}, u32[]{:S(2)}) %collective-permute-start.8) | collective-permute-done | bytes 2097184 | tf_op jit(solution)/shard_map/ppermute | solution.py:17
  217.4 6.1 %add_multiply_fusion = f32[1024,1024]{1,0:T(8,128)} fusion(bf16[1024,1024]{1,0:T(8,128)(2,1)} %collective-permute-done.9, bf16[1024,1024]{1,0:T(8,128)(2,1)} %collective-permute-done.8, f32[1024,1024]{1,0:T(8,128)S(1)} %fusion.12, f32[1024,1024]{1,0:T(8,128)S(1)} %fusion.7, f32[1024,1024]{1,0:T(8,128)S(1)} %fusion.11), kind=kLoop, calls=%fused_computation.6 | loop fusion | flops 7340032 | bytes 20971520 | tf_op jit(solution)/shard_map/mul | solution.py:114
  (6 shorter events, 0.0 us)
Async XLA Ops:
  0.6 96.3 %collective-permute-start = (bf16[1024,1024]{1,0:T(8,128)(2,1)}, bf16[1024,1024]{1,0:T(8,128)(2,1)S(1)}, u32[]{:S(2)}, u32[]{:S(2)}) collective-permute-start(bf16[1024,1024]{1,0:T(8,128)(2,1)} %param.3), channel_id=1, source_target_pairs={{1,0},{2,1},{3,2},{4,3},{5,4},{6,5},{7,6},{8,7},{9,8},{10,9},{11,1... | collective-permute-start | bytes 6291464 | tf_op jit(solution)/shard_map/ppermute | solution.py:17
  6.2 95.2 %collective-permute-start.1 = (bf16[1024,1024]{1,0:T(8,128)(2,1)}, bf16[1024,1024]{1,0:T(8,128)(2,1)}, u32[]{:S(2)}, u32[]{:S(2)}) collective-permute-start(bf16[1024,1024]{1,0:T(8,128)(2,1)} %param.3), channel_id=1, source_target_pairs={{9,0},{10,1},{11,2},{12,3},{13,4},{14,5},{15,6},{16,7},{17,8},{18,... | collective-permute-start | bytes 6291464 | tf_op jit(solution)/shard_map/ppermute | solution.py:17
  22.4 74.5 %copy-start.5 = (bf16[1024,1024]{1,0:T(8,128)(2,1)S(1)}, bf16[1024,1024]{1,0:T(8,128)(2,1)}, u32[]{:S(2)}) copy-start(bf16[1024,1024]{1,0:T(8,128)(2,1)} %param.3) | copy-start | bytes 6291460
  96.9 2.5 %copy-start.6 = (bf16[1024,1024]{1,0:T(8,128)(2,1)}, bf16[1024,1024]{1,0:T(8,128)(2,1)S(1)}, u32[]{:S(2)}) copy-start(bf16[1024,1024]{1,0:T(8,128)(2,1)S(1)} %collective-permute-done) | copy-start | bytes 6291460
  100.6 13.0 %collective-permute-start.2 = (f32[1024]{0:T(1024)S(1)}, f32[1024]{0:T(1024)S(1)}, u32[]{:S(2)}, u32[]{:S(2)}) collective-permute-start(f32[1024]{0:T(1024)S(1)} %get-tuple-element.3), channel_id=1, source_target_pairs={{127,0},{0,1},{1,2},{2,3},{3,4},{4,5},{5,6},{6,7},{7,8},{8,9},{9,1... | collective-permute-start | bytes 12296 | tf_op jit(solution)/shard_map/ppermute | solution.py:17
  105.5 2.4 %copy-start = (f32[1024,1024]{1,0:T(8,128)S(1)}, f32[1024,1024]{1,0:T(8,128)}, u32[]{:S(2)}) copy-start(f32[1024,1024]{1,0:T(8,128)} %copy.6) | copy-start | bytes 12582916
  106.6 9.2 %copy-start.2 = (f32[1024]{0:T(1024)S(1)}, f32[1024]{0:T(1024)}, u32[]{:S(2)}) copy-start(f32[1024]{0:T(1024)} %param.5) | copy-start | bytes 12292
  106.7 12.3 %copy-start.4 = (s32[1024]{0:T(1024)S(1)}, s32[1024]{0:T(1024)}, u32[]{:S(2)}) copy-start(s32[1024]{0:T(1024)} %param.4) | copy-start | bytes 12292
  107.4 8.5 %collective-permute-start.3 = (f32[1024]{0:T(1024)S(1)}, f32[1024]{0:T(1024)S(1)}, u32[]{:S(2)}, u32[]{:S(2)}) collective-permute-start(f32[1024]{0:T(1024)S(1)} %get-tuple-element.5), channel_id=1, source_target_pairs={{119,0},{120,1},{121,2},{122,3},{123,4},{124,5},{125,6},{126,7},{1... | collective-permute-start | bytes 12296 | tf_op jit(solution)/shard_map/ppermute | solution.py:17
  107.7 5.8 %collective-permute-start.4 = (f32[1024]{0:T(1024)S(1)}, f32[1024]{0:T(1024)S(1)}, u32[]{:S(2)}, u32[]{:S(2)}) collective-permute-start(f32[1024]{0:T(1024)S(1)} %exponential_reduce_fusion.1), channel_id=1, source_target_pairs={{127,0},{0,1},{1,2},{2,3},{3,4},{4,5},{5,6},{6,7},{7,8},{8,9},{9,1... | collective-permute-start | bytes 12296 | tf_op jit(solution)/shard_map/ppermute | solution.py:17
  107.8 8.1 %collective-permute-start.5 = (f32[1024]{0:T(1024)S(1)}, f32[1024]{0:T(1024)S(1)}, u32[]{:S(2)}, u32[]{:S(2)}) collective-permute-start(f32[1024]{0:T(1024)S(1)} %exponential_reduce_fusion), channel_id=1, source_target_pairs={{119,0},{120,1},{121,2},{122,3},{123,4},{124,5},{125,6},{126,7},{1... | collective-permute-start | bytes 12296 | tf_op jit(solution)/shard_map/ppermute | solution.py:17
  115.9 20.3 %copy-start.3 = (f32[1024]{0:T(1024)}, f32[1024]{0:T(1024)S(1)}, u32[]{:S(2)}) copy-start(f32[1024]{0:T(1024)S(1)} %log_add_fusion) | copy-start | bytes 12292
  115.9 5.7 %collective-permute-start.7 = (f32[1024]{0:T(1024)S(1)}, f32[1024]{0:T(1024)S(1)}, u32[]{:S(2)}, u32[]{:S(2)}) collective-permute-start(f32[1024]{0:T(1024)S(1)} %log_add_fusion), channel_id=1, source_target_pairs={{9,0},{10,1},{11,2},{12,3},{13,4},{14,5},{15,6},{16,7},{17,8},{18,... | collective-permute-start | bytes 12296 | tf_op jit(solution)/shard_map/ppermute | solution.py:17
  119.0 7.6 %collective-permute-start.6 = (f32[1024]{0:T(1024)S(1)}, f32[1024]{0:T(1024)S(1)}, u32[]{:S(2)}, u32[]{:S(2)}) collective-permute-start(f32[1024]{0:T(1024)S(1)} %log_add_fusion), channel_id=1, source_target_pairs={{1,0},{2,1},{3,2},{4,3},{5,4},{6,5},{7,6},{8,7},{9,8},{10,9},{11,1... | collective-permute-start | bytes 12296 | tf_op jit(solution)/shard_map/ppermute | solution.py:17
  124.6 5.3 %copy-start.1 = (f32[1024,1024]{0,1:T(8,128)S(1)}, f32[1024,1024]{0,1:T(8,128)}, u32[]{:S(2)}) copy-start(f32[1024,1024]{0,1:T(8,128)} %convolution_multiply_fusion) | copy-start | bytes 12582916
  124.6 51.3 %collective-permute-start.9 = (bf16[1024,1024]{1,0:T(8,128)(2,1)S(1)}, bf16[1024,1024]{1,0:T(8,128)(2,1)}, u32[]{:S(2)}, u32[]{:S(2)}) collective-permute-start(bf16[1024,1024]{1,0:T(8,128)(2,1)S(1)} %convolution_convert_fusion), channel_id=1, source_target_pairs={{119,0},{120,1},{121,2},{122,3},{123,4},{124,5},{125,6},{126,7},{1... | collective-permute-start | bytes 6291464 | tf_op jit(solution)/shard_map/ppermute | solution.py:17
  129.5 3.9 %copy-start.7 = (bf16[1024,1024]{1,0:T(8,128)(2,1)S(1)}, bf16[1024,1024]{1,0:T(8,128)(2,1)}, u32[]{:S(2)}) copy-start(bf16[1024,1024]{1,0:T(8,128)(2,1)} %copy-done.6) | copy-start | bytes 6291460
  129.6 87.8 %collective-permute-start.8 = (bf16[1024,1024]{1,0:T(8,128)(2,1)S(1)}, bf16[1024,1024]{1,0:T(8,128)(2,1)}, u32[]{:S(2)}, u32[]{:S(2)}) collective-permute-start(bf16[1024,1024]{1,0:T(8,128)(2,1)S(1)} %convolution_convert_fusion.1), channel_id=1, source_target_pairs={{127,0},{0,1},{1,2},{2,3},{3,4},{4,5},{5,6},{6,7},{7,8},{8,9},{9,1... | collective-permute-start | bytes 6291464 | tf_op jit(solution)/shard_map/ppermute | solution.py:17
where the time goes:
time: 224 us; the launch traced here: 223 us
  waiting for transfers between devices  156 us (70%)
  matrix products  29.7 us (13%)
  starting transfers between devices  18.3 us (8%)
  other arithmetic  13.4 us (6%)
  local copies, waits for them, and re-layouts  5.39 us (2%)
    ppermute x10, waiting for transfers between devices, passed_along(): return lax.ppermute(block, axis, route)  156 us
    ppermute x10, starting transfers between devices, passed_along(): return lax.ppermute(block, axis, route)  18.3 us
    dot_general x3, matrix products, similarity(): lax.dot_general(left, right, (((1,), (1,)), ((), ())), preferred_element_...  13.2 us
    mul x1, other arithmetic, per_device(): return (SCALE * gradient, row_lse)  6.1 us
    dot_general x2, matrix products, transposed_product(): lax.dot_general(weights, block, (((0,), (0,)), ((), ())), preferred_eleme...  5.85 us
    mul x1, local copies, waits for them, and re-layouts, similarity(): SCALE * lax.dot_general(left, right, (((1,), (1,)), ((), ())), preferred_...  5.35 us
  transfers between devices with their start and end apart: 10, of which 5 were waited for; matrix products, arithmetic and copies ran while one was open for 19% of the time, Pallas kernels for 0%

commit v1 on v0

v1 whole, which is shorter than its diff:
```python
import functools
import math

import jax
import jax.numpy as jnp
from jax import lax
from jax.experimental import pallas as pl
from jax.experimental.pallas import tpu as pltpu
from jax.sharding import PartitionSpec as P

MESH = pl.DeviceIdType.MESH
BLOCKS = 128
ROWS = 1024
D = 1024
SCALE = 20.0
LOG2E = math.log2(math.e)
LN2 = math.log(2.0)
CHUNKS = 16
R = ROWS // CHUNKS
GROUP = 256
PER_GROUP = GROUP // R
LAG = 5
BEHIND = 8
MASKED = -1e37
M1, P1, M9, P9, RL, RZ = range(6)


def coords(b):
    dp, sub = b // 8, b % 8
    return dp // 4, sub % 4, (dp // 2) % 2 * 2 + sub // 4, dp % 2


def block_at(x, y, z, c):
    return ((x * 2 + z // 2) * 2 + c) * 8 + (z % 2) * 4 + y


def device(b):
    return (b // 8, b % 8)


def core(b):
    return (b // 8) % 2


def near(b, step):
    return (b + BLOCKS + step) % BLOCKS


def in_column(b, y):
    x, _, z, c = coords(b)
    return block_at(x, y, z, c)


def kernel(
    e_hbm, partner_ref, prior_ref, grad_hbm, lse_ref,
    own, buf, scores, out, peak, total, lcol, pcol, lnb,
    load_sem, store_sem, s_up, s_dn, s_far, s_r9, s_r1, s_z, s_loc, s_lse, r_lse, recv,
):
    b = lax.axis_index("dp") * 8 + lax.axis_index("sub")
    x, y, z, c = coords(b)
    up, dn = block_at(x, (y + 1) % 4, z, c), block_at(x, (y + 3) % 4, z, c)
    mate = block_at(x, y, z, 1 - c)
    y0, y3 = y == 0, y == 3

    load = pltpu.make_async_copy(e_hbm, own, load_sem)
    load.start()

    barrier = pltpu.get_barrier_semaphore()

    def greet(t):
        pl.semaphore_signal(barrier, inc=1, device_id=device(t), device_id_type=MESH)

    for t in (up, dn, near(b, 1), near(b, -1), near(b, 9), near(b, -9), near(b, 8), near(b, -8)):
        greet(t)

    @pl.when(y0)
    def _():
        greet(in_column(near(b, -1), 0))
        greet(in_column(near(b, -9), 0))
        greet(in_column(near(b, -1), 0))
        greet(near(in_column(b, 3), 1))

    @pl.when(y3)
    def _():
        greet(in_column(near(b, 1), 3))
        greet(in_column(near(b, 9), 3))
        greet(in_column(near(b, 1), 3))
        greet(near(in_column(b, 0), -1))

    pl.semaphore_wait(barrier, 8 + jnp.where(y0 | y3, 4, 0))

    up_dbl, up_sgl = y3 & (core(near(b, 1)) == 1), y3 & (core(near(b, 1)) == 0)
    dn_dbl, dn_sgl = y0 & (core(near(b, -1)) == 0), y0 & (core(near(b, -1)) == 1)
    q1 = jnp.where(y0, near(dn, 1), near(up, -1))
    q9 = jnp.where(y0, near(dn, 9), near(up, -9))
    wrap = y0 | y3
    rel_dbl = (y0 & (core(q1) == 1)) | (y3 & (core(q1) == 0))
    rel_sgl = wrap & ~rel_dbl
    rel_z = (y3 & (c == 0)) | (y0 & (c == 1))
    do_far = ((~y0) & (c == 1)) | ((~y3) & (c == 0))
    loc_late = (y0 & (c == 0)) | (y3 & (c == 1))
    near_slot, far_slot = jnp.where(y0, M1, P1), jnp.where(y0, M9, P9)

    def rows(k):
        return pl.ds(pl.multiple_of(k * R, R), R)

    def copy(src, to, slot, k, sem):
        return pltpu.make_async_remote_copy(
            src_ref=src, dst_ref=buf.at[slot, rows(k)], send_sem=sem, recv_sem=recv.at[slot, k],
            device_id=device(to), device_id_type=MESH,
        )

    def held(slot, k):
        return buf.at[slot, rows(k)]

    def arrived(slot, k):
        pltpu.make_async_copy(held(slot, k), held(slot, k), recv.at[slot, k]).wait()

    def send_up(k):
        odd = k % 2 == 1
        to = jnp.where(up_sgl & odd, in_column(near(b, 1), 3), up)
        slot = jnp.where(y3, jnp.where(up_sgl & odd, RZ, RL), M1)
        return copy(e_hbm.at[rows(k)], to, slot, k, s_up.at[k])

    def send_dn(k):
        odd = k % 2 == 1
        to = jnp.where(dn_sgl & odd, in_column(near(b, -1), 0), dn)
        slot = jnp.where(y0, jnp.where(dn_sgl & odd, RZ, RL), P1)
        return copy(e_hbm.at[rows(k)], to, slot, k, s_dn.at[k])

    def send_far(k):
        return copy(
            held(jnp.where(c == 1, M1, P1), k), jnp.where(c == 1, near(b, 8), near(b, -8)),
            jnp.where(c == 1, M9, P9), k, s_far.at[k],
        )

    def send_r1(k):
        return copy(held(RL, k), q1, near_slot, k, s_r1.at[k])

    def send_r9(k):
        return copy(held(RL, k), q9, far_slot, k, s_r9.at[k])

    def send_z(k):
        return copy(held(RZ, k), jnp.where(y3, up, dn), jnp.where(y3, M1, P1), k, s_z.at[k])

    def send_loc(k):
        return copy(held(jnp.where(c == 0, M1, P1), k), mate, jnp.where(c == 0, M9, P9), k, s_loc.at[k])

    def start_own(k, carry):
        send_up(k).start()
        send_dn(k).start()
        return carry

    lax.fori_loop(0, CHUNKS, start_own, 0)

    load.wait()

    def column(row):
        return jnp.transpose(jnp.broadcast_to(row, (128, ROWS)))

    pcol[...] = column((partner_ref[...] % ROWS).astype(jnp.float32))

    def scored(left, right):
        return (SCALE * LOG2E) * lax.dot_general(
            left, right, (((1,), (1,)), ((), ())), preferred_element_type=jnp.float32
        )

    def own_scores(g, carry):
        cols = pl.ds(pl.multiple_of(g * GROUP, GROUP), GROUP)
        tile = scored(own[...], own[cols, :])
        diagonal = lax.broadcasted_iota(jnp.int32, tile.shape, 0) == (
            lax.broadcasted_iota(jnp.int32, tile.shape, 1) + g * GROUP
        )
        scores[4, :, cols] = jnp.where(diagonal, MASKED, tile)
        return carry

    lax.fori_loop(0, ROWS // GROUP, own_scores, 0)

    def own_stats(r, carry):
        at = pl.ds(pl.multiple_of(r * 64, 64), 64)
        top = scores[4, at, 0:128]
        for i in range(1, 8):
            top = jnp.maximum(top, scores[4, at, i * 128 : (i + 1) * 128])
        acc = jnp.exp2(scores[4, at, 0:128] - top)
        for i in range(1, 8):
            acc = acc + jnp.exp2(scores[4, at, i * 128 : (i + 1) * 128] - top)
        peak[at, :] = top
        total[at, :] = acc
        return carry

    lax.fori_loop(0, ROWS // 64, own_stats, 0)

    def step(k, carry):
        @pl.when(k < CHUNKS)
        def _():
            odd = k % 2 == 1

            @pl.when(rel_dbl)
            def _():
                arrived(RL, k)
                send_r1(k).start()
                send_r9(k).start()

            @pl.when(rel_sgl & ~odd)
            def _():
                arrived(RL, k)
                send_r1(k).start()

            @pl.when(rel_z & odd)
            def _():
                arrived(RZ, k)
                send_z(k).start()

            @pl.when(~y0)
            def _():
                arrived(M1, k)

            @pl.when(~y3)
            def _():
                arrived(P1, k)

            @pl.when(do_far)
            def _():
                send_far(k).start()

            @pl.when(~loc_late)
            def _():
                send_loc(k).start()

        @pl.when((k >= LAG) & (k < CHUNKS + LAG))
        def _():
            j = k - LAG

            @pl.when(y0)
            def _():
                arrived(M1, j)

            @pl.when(y3)
            def _():
                arrived(P1, j)

            @pl.when(loc_late)
            def _():
                send_loc(j).start()

        @pl.when(k >= BEHIND)
        def _():
            item = k - BEHIND
            g, t = item // 4, item % 4

            @pl.when(t >= 2)
            def _():
                for i in range(PER_GROUP):
                    arrived(t, g * PER_GROUP + i)

            cols = pl.ds(pl.multiple_of(g * GROUP, GROUP), GROUP)
            scores[t, :, cols] = scored(own[...], buf[t, cols, :])

            def stats(r, carry):
                at = pl.ds(pl.multiple_of(r * 128, 128), 128)
                tile = scores[t, at, cols]
                old = peak[at, :]
                top = jnp.maximum(old, jnp.maximum(tile[:, :128], tile[:, 128:]))
                peak[at, :] = top
                total[at, :] = (
                    total[at, :] * jnp.exp2(old - top) + jnp.exp2(tile[:, :128] - top) + jnp.exp2(tile[:, 128:] - top)
                )
                return carry

            lax.fori_loop(0, ROWS // 128, stats, 0, unroll=2)

        return carry

    lax.fori_loop(0, CHUNKS + BEHIND, step, 0)

    prior = column(prior_ref[...] * LOG2E)
    lane_peak = peak[...]
    top = jnp.broadcast_to(jnp.max(lane_peak, axis=1, keepdims=True), (ROWS, 128))
    summed = jnp.sum(total[...] * jnp.exp2(lane_peak - top), axis=1, keepdims=True)
    both = jnp.maximum(top, prior)
    lse2 = both + jnp.log2(summed * jnp.exp2(top - both) + jnp.exp2(prior - both))
    lcol[...] = lse2
    lnb[4] = jnp.transpose(lse2)[0:8, :]
    lse_ref[...] = lnb[4, 0:1, :] * LN2

    def send_lse(t, to):
        return pltpu.make_async_remote_copy(
            src_ref=lnb.at[4], dst_ref=lnb.at[t], send_sem=s_lse.at[t], recv_sem=r_lse.at[t],
            device_id=device(to), device_id_type=MESH,
        )

    lse_sends = [send_lse(M1, near(b, 1)), send_lse(P1, near(b, -1)), send_lse(M9, near(b, 9)), send_lse(P9, near(b, -9))]
    for s in lse_sends:
        s.start()

    def weights(t, at):
        parts = []
        mine = lcol[at, :]
        for i in range(8):
            lanes = slice(i * 128, (i + 1) * 128)
            tile = scores[t, at, lanes]
            parts.append(jnp.exp2(tile - mine) + jnp.exp2(tile - lnb[t, 0:1, lanes]))
        return parts

    prow = (partner_ref[...] % ROWS).astype(jnp.float32)

    def own_part(r, carry):
        at = pl.ds(pl.multiple_of(r * 256, 256), 256)
        parts = weights(4, at)
        mine = pcol[at, :]
        row = (lax.broadcasted_iota(jnp.int32, (256, 128), 0) + r * 256).astype(jnp.float32)
        lane = lax.broadcasted_iota(jnp.int32, (256, 128), 1).astype(jnp.float32)
        for i in range(8):
            lanes = slice(i * 128, (i + 1) * 128)
            hot = jnp.where(mine == lane + i * 128.0, 1.0, 0.0) + jnp.where(prow[:, lanes] == row, 1.0, 0.0)
            parts[i] = (parts[i] - hot).astype(jnp.bfloat16)
        out[at, :] = jnp.dot(jnp.concatenate(parts, axis=1), own[...], preferred_element_type=jnp.float32)
        return carry

    lax.fori_loop(0, 4, own_part, 0)

    for s in lse_sends:
        s.wait_recv()

    def rest(r, carry):
        at = pl.ds(pl.multiple_of(r * 256, 256), 256)
        acc = out[at, :]
        for t in (P1, P9, M1, M9):
            w = jnp.concatenate([p.astype(jnp.bfloat16) for p in weights(t, at)], axis=1)
            term = jnp.dot(w, buf[t], preferred_element_type=jnp.float32)
            if t in (M1, M9):
                term = term.astype(jnp.bfloat16).astype(jnp.float32)
            acc = acc + term
        out[at, :] = SCALE * acc
        pltpu.make_async_copy(out.at[at], grad_hbm.at[at], store_sem.at[r]).start()
        return carry

    lax.fori_loop(0, 4, rest, 0)

    for s in lse_sends:
        s.wait_send()

    def sent(k, carry):
        odd = k % 2 == 1
        send_up(k).wait_send()
        send_dn(k).wait_send()
        send_loc(k).wait_send()

        @pl.when(do_far)
        def _():
            send_far(k).wait_send()

        @pl.when(rel_dbl)
        def _():
            send_r1(k).wait_send()
            send_r9(k).wait_send()

        @pl.when(rel_sgl & ~odd)
        def _():
            send_r1(k).wait_send()

        @pl.when(rel_z & odd)
        def _():
            send_z(k).wait_send()

        return carry

    lax.fori_loop(0, CHUNKS, sent, 0)

    def stored(r, carry):
        at = pl.ds(pl.multiple_of(r * 256, 256), 256)
        pltpu.make_async_copy(out.at[at], grad_hbm.at[at], store_sem.at[r]).wait()
        return carry

    lax.fori_loop(0, 4, stored, 0)


def per_device(embeddings, partner, prior_lse):
    dma = pltpu.SemaphoreType.DMA
    f32 = jnp.float32
    gradient, lse = pl.pallas_call(
        kernel,
        out_shape=(jax.ShapeDtypeStruct((ROWS, D), f32), jax.ShapeDtypeStruct((1, ROWS), f32)),
        in_specs=[
            pl.BlockSpec(memory_space=pl.ANY),
            pl.BlockSpec(memory_space=pltpu.VMEM),
            pl.BlockSpec(memory_space=pltpu.VMEM),
        ],
        out_specs=(pl.BlockSpec(memory_space=pl.ANY), pl.BlockSpec(memory_space=pltpu.VMEM)),
        scratch_shapes=[
            pltpu.VMEM((ROWS, D), jnp.bfloat16),
            pltpu.VMEM((6, ROWS, D), jnp.bfloat16),
            pltpu.VMEM((5, ROWS, ROWS), f32),
            pltpu.VMEM((ROWS, D), f32),
            pltpu.VMEM((ROWS, 128), f32),
            pltpu.VMEM((ROWS, 128), f32),
            pltpu.VMEM((ROWS, 128), f32),
            pltpu.VMEM((ROWS, 128), f32),
            pltpu.VMEM((5, 8, ROWS), f32),
            dma, dma((4,)), dma((CHUNKS,)), dma((CHUNKS,)), dma((CHUNKS,)), dma((CHUNKS,)), dma((CHUNKS,)),
            dma((CHUNKS,)), dma((CHUNKS,)), dma((4,)), dma((4,)), dma((6, CHUNKS)),
        ],
        compiler_params=pltpu.CompilerParams(collective_id=0, has_side_effects=True, vmem_limit_bytes=56 << 20),
        cost_estimate=pl.CostEstimate(flops=20 * ROWS * ROWS * D, bytes_accessed=8 << 20, transcendentals=20 << 20),
    )(embeddings, partner.reshape(1, ROWS), prior_lse.reshape(1, ROWS))
    return gradient, lse.reshape(ROWS)


def solution(mesh):
    placed = (P(("dp", "sub"), None), P(("dp", "sub")), P(("dp", "sub")))
    return jax.shard_map(
        per_device,
        mesh=mesh,
        in_specs=placed,
        out_specs=(P(("dp", "sub"), None), P(("dp", "sub"))),
        check_vma=False,
    )
```

time: 224 us -> 106 us (0.47)
  the two profiles are of different devices: /device:TPU:1 before, /device:TPU:0 now
where the time goes in v1:
time: 106 us; the launch traced here: 105 us
  Pallas kernels  99.4 us (94%)
  local copies, waits for them, and re-layouts  5.39 us (5%)
    pallas_call x1, Pallas kernels, per_device(): pl.pallas_call(kernel, out_shape=(jax.ShapeDtypeStruct((ROWS, D), f32), j...  99.4 us
    unnamed x4, local copies, waits for them, and re-layouts  5.39 us

profile of v1, /device:TPU:0, one launch (start us, length us, event | category | flops | bytes accessed | tf_op | source)
XLA Modules:
  0.0 105.5 jit_solution(17192936013543854293)
XLA Ops:
  0.6 99.4 %shard_map.50 = (f32[1024,1024]{1,0:T(8,128)}, f32[1,1024]{1,0:T(1,128)}) custom-call(bf16[1024,1024]{1,0:T(8,128)(2,1)} %e_hbm.1, s32[1,1024]{1,0:T(1,128)} %bitcast.4, f32[1,1024]{1,0:T(1,128)} %bitcast.5), custom_call_target="tpu_custom_call" | custom-call | flops 21474836480 | bytes 8388608 | tf_op jit(solution)/shard_map/pallas_call | solution.py:381
  100.1 0.0 copy-start
  100.1 4.8 %copy.7 = f32[1024,1024]{1,0:T(8,128)} copy(f32[1024,1024]{1,0:T(8,128)} %get-tuple-element.8) | data formatting | bytes 8388608
  104.9 0.0 copy-done
  104.9 0.6 copy.8
Async XLA Ops:
  100.1 4.8 %copy-start = (f32[1,1024]{1,0:T(1,128)S(1)}, f32[1,1024]{1,0:T(1,128)}, u32[]{:S(2)}) copy-start(f32[1,1024]{1,0:T(1,128)} %get-tuple-element.5) | copy-start | bytes 12292

commit v2 on v1

--- a/solution.py
+++ b/solution.py
@@ -70,7 +70,7 @@
     def greet(t):
         pl.semaphore_signal(barrier, inc=1, device_id=device(t), device_id_type=MESH)
 
-    for t in (up, dn, near(b, 1), near(b, -1), near(b, 9), near(b, -9), near(b, 8), near(b, -8)):
+    for t in (up, dn, mate, near(b, 16 * c - 8)):
         greet(t)
 
     @pl.when(y0)
@@ -87,7 +87,14 @@
         greet(in_column(near(b, 1), 3))
         greet(near(in_column(b, 0), -1))
 
-    pl.semaphore_wait(barrier, 8 + jnp.where(y0 | y3, 4, 0))
+    z_src = ((y == 1) & (c == 0)) | ((y == 2) & (c == 1))
+    z_mid = ((y == 1) & (c == 1)) | ((y == 2) & (c == 0))
+
+    @pl.when(z_mid)
+    def _():
+        greet(jnp.where(y == 1, near(in_column(b, 0), 9), near(in_column(b, 3), -9)))
+
+    pl.semaphore_wait(barrier, 4 + jnp.where(y0 | y3, 4, 0) + jnp.where(z_src, 1, 0))
 
     up_dbl, up_sgl = y3 & (core(near(b, 1)) == 1), y3 & (core(near(b, 1)) == 0)
     dn_dbl, dn_sgl = y0 & (core(near(b, -1)) == 0), y0 & (core(near(b, -1)) == 1)
@@ -141,12 +148,28 @@
         return copy(held(RL, k), q9, far_slot, k, s_r9.at[k])
 
     def send_z(k):
-        return copy(held(RZ, k), jnp.where(y3, up, dn), jnp.where(y3, M1, P1), k, s_z.at[k])
+        ahead = (y == 0) | (y == 1)
+        slot = jnp.where(y3, M1, jnp.where(y0, P1, jnp.where(y == 1, P9, M9)))
+        return copy(held(RZ, k), jnp.where(ahead, dn, up), slot, k, s_z.at[k])
+
+    def send_side(k):
+        to = jnp.where(y == 1, in_column(near(b, -9), 1), in_column(near(b, 9), 2))
+        return copy(e_hbm.at[rows(k)], to, RZ, k, s_z.at[k])
 
     def send_loc(k):
         return copy(held(jnp.where(c == 0, M1, P1), k), mate, jnp.where(c == 0, M9, P9), k, s_loc.at[k])
 
+    def z_moves(k):
+        return (rel_z & (k % 2 == 1)) | (z_mid & (k % 4 == 3))
+
+    def far_moves(k):
+        return do_far & ~(wrap & (k % 4 == 3))
+
     def start_own(k, carry):
+        @pl.when(z_src & (k % 4 == 3))
+        def _():
+            send_side(k).start()
+
         send_up(k).start()
         send_dn(k).start()
         return carry
@@ -206,7 +229,7 @@
                 arrived(RL, k)
                 send_r1(k).start()
 
-            @pl.when(rel_z & odd)
+            @pl.when(z_moves(k))
             def _():
                 arrived(RZ, k)
                 send_z(k).start()
@@ -219,7 +242,7 @@
             def _():
                 arrived(P1, k)
 
-            @pl.when(do_far)
+            @pl.when(far_moves(k))
             def _():
                 send_far(k).start()
 
@@ -346,7 +369,7 @@
         send_dn(k).wait_send()
         send_loc(k).wait_send()
 
-        @pl.when(do_far)
+        @pl.when(far_moves(k))
         def _():
             send_far(k).wait_send()
 
@@ -359,7 +382,11 @@
         def _():
             send_r1(k).wait_send()
 
-        @pl.when(rel_z & odd)
+        @pl.when(z_src & (k % 4 == 3))
+        def _():
+            send_side(k).wait_send()
+
+        @pl.when(z_moves(k))
         def _():
             send_z(k).wait_send()
 
@@ -380,7 +407,7 @@
     f32 = jnp.float32
     gradient, lse = pl.pallas_call(
         kernel,
-        out_shape=(jax.ShapeDtypeStruct((ROWS, D), f32), jax.ShapeDtypeStruct((1, ROWS), f32)),
+        out_shape=(pltpu.VMEM((ROWS, D), f32), jax.ShapeDtypeStruct((1, ROWS), f32)),
         in_specs=[
             pl.BlockSpec(memory_space=pl.ANY),
             pl.BlockSpec(memory_space=pltpu.VMEM),

time: 106 us -> 98.6 us (0.930)
  the two profiles are of different devices: /device:TPU:0 before, /device:TPU:1 now
where the time goes in v2:
time: 98.6 us; the launch traced here: 98.4 us
  Pallas kernels  95.2 us (97%)
  local copies, waits for them, and re-layouts  2.61 us (3%)
    pallas_call x1, Pallas kernels, per_device(): pl.pallas_call(kernel, out_shape=(pltpu.VMEM((ROWS, D), f32), jax.ShapeDt...  95.2 us
    unnamed x4, local copies, waits for them, and re-layouts  2.61 us

profile of v2, /device:TPU:1, one launch (start us, length us, event | category | flops | bytes accessed | tf_op | source)
XLA Modules:
  0.0 98.4 jit_solution(14354748252254322635)
XLA Ops:
  0.6 95.2 %shard_map.50 = (f32[1024,1024]{1,0:T(8,128)S(1)}, f32[1,1024]{1,0:T(1,128)}) custom-call(bf16[1024,1024]{1,0:T(8,128)(2,1)} %e_hbm.1, s32[1,1024]{1,0:T(1,128)} %bitcast.4, f32[1,1024]{1,0:T(1,128)} %bitcast.5), custom_call_target="tpu_custom_call" | custom-call | flops 21474836480 | bytes 8388608 | tf_op jit(solution)/shard_map/pallas_call | solution.py:408
  95.8 0.0 copy-start
  95.8 2.0 %copy.7 = f32[1024,1024]{1,0:T(8,128)} copy(f32[1024,1024]{1,0:T(8,128)S(1)} %get-tuple-element.6) | data formatting | bytes 8388608
  97.8 0.0 copy-done
  97.8 0.6 copy.8
Async XLA Ops:
  95.8 2.0 %copy-start = (f32[1,1024]{1,0:T(1,128)S(1)}, f32[1,1024]{1,0:T(1,128)}, u32[]{:S(2)}) copy-start(f32[1,1024]{1,0:T(1,128)} %get-tuple-element.5) | copy-start | bytes 12292

commit v3 on v2

--- a/solution.py
+++ b/solution.py
@@ -16,11 +16,13 @@
 LOG2E = math.log2(math.e)
 LN2 = math.log(2.0)
 CHUNKS = 16
+AHEAD = 4
+PACE = CHUNKS // 16
 R = ROWS // CHUNKS
 GROUP = 256
 PER_GROUP = GROUP // R
-LAG = 5
-BEHIND = 8
+LAG = 5 * PACE
+BEHIND = 8 * PACE
 MASKED = -1e37
 M1, P1, M9, P9, RL, RZ = range(6)
 
@@ -165,55 +167,49 @@
     def far_moves(k):
         return do_far & ~(wrap & (k % 4 == 3))
 
-    def start_own(k, carry):
+    def start_own(k):
         @pl.when(z_src & (k % 4 == 3))
         def _():
             send_side(k).start()
 
         send_up(k).start()
         send_dn(k).start()
-        return carry
-
-    lax.fori_loop(0, CHUNKS, start_own, 0)
-
-    load.wait()
+
+    for k in range(AHEAD):
+        start_own(k)
 
     def column(row):
         return jnp.transpose(jnp.broadcast_to(row, (128, ROWS)))
-
-    pcol[...] = column((partner_ref[...] % ROWS).astype(jnp.float32))
 
     def scored(left, right):
         return (SCALE * LOG2E) * lax.dot_general(
             left, right, (((1,), (1,)), ((), ())), preferred_element_type=jnp.float32
         )
 
-    def own_scores(g, carry):
-        cols = pl.ds(pl.multiple_of(g * GROUP, GROUP), GROUP)
-        tile = scored(own[...], own[cols, :])
-        diagonal = lax.broadcasted_iota(jnp.int32, tile.shape, 0) == (
-            lax.broadcasted_iota(jnp.int32, tile.shape, 1) + g * GROUP
-        )
-        scores[4, :, cols] = jnp.where(diagonal, MASKED, tile)
-        return carry
-
-    lax.fori_loop(0, ROWS // GROUP, own_scores, 0)
-
-    def own_stats(r, carry):
-        at = pl.ds(pl.multiple_of(r * 64, 64), 64)
-        top = scores[4, at, 0:128]
-        for i in range(1, 8):
-            top = jnp.maximum(top, scores[4, at, i * 128 : (i + 1) * 128])
-        acc = jnp.exp2(scores[4, at, 0:128] - top)
-        for i in range(1, 8):
-            acc = acc + jnp.exp2(scores[4, at, i * 128 : (i + 1) * 128] - top)
-        peak[at, :] = top
-        total[at, :] = acc
-        return carry
-
-    lax.fori_loop(0, ROWS // 64, own_stats, 0)
+    peak[...] = jnp.full((ROWS, 128), 10 * MASKED)
+    total[...] = jnp.zeros((ROWS, 128), jnp.float32)
+
+    def gather_stats(t, cols):
+        def stats(r, carry):
+            at = pl.ds(pl.multiple_of(r * 128, 128), 128)
+            tile = scores[t, at, cols]
+            old = peak[at, :]
+            top = jnp.maximum(old, jnp.maximum(tile[:, :128], tile[:, 128:]))
+            peak[at, :] = top
+            total[at, :] = (
+                total[at, :] * jnp.exp2(old - top) + jnp.exp2(tile[:, :128] - top) + jnp.exp2(tile[:, 128:] - top)
+            )
+            return carry
+
+        lax.fori_loop(0, ROWS // 128, stats, 0, unroll=2)
 
     def step(k, carry):
+        @pl.when(k + AHEAD < CHUNKS)
+        def _():
+            send_up(k).wait_send()
+            send_dn(k).wait_send()
+            start_own(k + AHEAD)
+
         @pl.when(k < CHUNKS)
         def _():
             odd = k % 2 == 1
@@ -266,9 +262,20 @@
             def _():
                 send_loc(j).start()
 
-        @pl.when(k >= BEHIND)
-        def _():
-            item = k - BEHIND
+        @pl.when((k % PACE == 0) & (k < 4 * PACE))
+        def _():
+            g = k // PACE
+            cols = pl.ds(pl.multiple_of(g * GROUP, GROUP), GROUP)
+            tile = scored(own[...], own[cols, :])
+            diagonal = lax.broadcasted_iota(jnp.int32, tile.shape, 0) == (
+                lax.broadcasted_iota(jnp.int32, tile.shape, 1) + g * GROUP
+            )
+            scores[4, :, cols] = jnp.where(diagonal, MASKED, tile)
+            gather_stats(4, cols)
+
+        @pl.when((k % PACE == 0) & (k >= BEHIND))
+        def _():
+            item = (k - BEHIND) // PACE
             g, t = item // 4, item % 4
 
             @pl.when(t >= 2)
@@ -278,22 +285,11 @@
 
             cols = pl.ds(pl.multiple_of(g * GROUP, GROUP), GROUP)
             scores[t, :, cols] = scored(own[...], buf[t, cols, :])
-
-            def stats(r, carry):
-                at = pl.ds(pl.multiple_of(r * 128, 128), 128)
-                tile = scores[t, at, cols]
-                old = peak[at, :]
-                top = jnp.maximum(old, jnp.maximum(tile[:, :128], tile[:, 128:]))
-                peak[at, :] = top
-                total[at, :] = (
-                    total[at, :] * jnp.exp2(old - top) + jnp.exp2(tile[:, :128] - top) + jnp.exp2(tile[:, 128:] - top)
-                )
-                return carry
-
-            lax.fori_loop(0, ROWS // 128, stats, 0, unroll=2)
+            gather_stats(t, cols)
 
         return carry
 
+    load.wait()
     lax.fori_loop(0, CHUNKS + BEHIND, step, 0)
 
     prior = column(prior_ref[...] * LOG2E)
@@ -326,6 +322,7 @@
         return parts
 
     prow = (partner_ref[...] % ROWS).astype(jnp.float32)
+    pcol[...] = column(prow)
 
     def own_part(r, carry):
         at = pl.ds(pl.multiple_of(r * 256, 256), 256)
@@ -365,8 +362,11 @@
 
     def sent(k, carry):
         odd = k % 2 == 1
-        send_up(k).wait_send()
-        send_dn(k).wait_send()
+        @pl.when(k + AHEAD >= CHUNKS)
+        def _():
+            send_up(k).wait_send()
+            send_dn(k).wait_send()
+
         send_loc(k).wait_send()
 
         @pl.when(far_moves(k))

time: 98.6 us -> 92.7 us (0.940)
  Pallas kernels: 95.2 us -> 89.3 us
    pallas_call x1, Pallas kernels: 95.2 us -> 89.3 us  [per_device(): pl.pallas_call(kernel, out_shape=(pltpu.VMEM((ROWS, D), f32), jax.ShapeDt...]
where the time goes in v3:
time: 92.7 us; the launch traced here: 92.6 us
  Pallas kernels  89.3 us (96%)
  local copies, waits for them, and re-layouts  2.61 us (3%)
    pallas_call x1, Pallas kernels, per_device(): pl.pallas_call(kernel, out_shape=(pltpu.VMEM((ROWS, D), f32), jax.ShapeDt...  89.3 us
    unnamed x4, local copies, waits for them, and re-layouts  2.61 us

profile of v3, /device:TPU:1, one launch (start us, length us, event | category | flops | bytes accessed | tf_op | source)
XLA Modules:
  0.0 92.6 jit_solution(11305177382006382472)
XLA Ops:
  0.6 89.3 %shard_map.50 = (f32[1024,1024]{1,0:T(8,128)S(1)}, f32[1,1024]{1,0:T(1,128)}) custom-call(bf16[1024,1024]{1,0:T(8,128)(2,1)} %e_hbm.1, s32[1,1024]{1,0:T(1,128)} %bitcast.4, f32[1,1024]{1,0:T(1,128)} %bitcast.5), custom_call_target="tpu_custom_call" | custom-call | flops 21474836480 | bytes 8388608 | tf_op jit(solution)/shard_map/pallas_call | solution.py:408
  90.0 0.0 copy-start
  90.0 2.0 %copy.7 = f32[1024,1024]{1,0:T(8,128)} copy(f32[1024,1024]{1,0:T(8,128)S(1)} %get-tuple-element.6) | data formatting | bytes 8388608
  92.0 0.0 copy-done
  92.0 0.6 copy.8
Async XLA Ops:
  90.0 2.0 %copy-start = (f32[1,1024]{1,0:T(1,128)S(1)}, f32[1,1024]{1,0:T(1,128)}, u32[]{:S(2)}) copy-start(f32[1,1024]{1,0:T(1,128)} %get-tuple-element.5) | copy-start | bytes 12292

commit v4 on v3

--- a/solution.py
+++ b/solution.py
@@ -21,8 +21,8 @@
 R = ROWS // CHUNKS
 GROUP = 256
 PER_GROUP = GROUP // R
-LAG = 5 * PACE
-BEHIND = 8 * PACE
+LAG = 2 * PACE
+BEHIND = 5 * PACE
 MASKED = -1e37
 M1, P1, M9, P9, RL, RZ = range(6)
 
@@ -53,10 +53,14 @@
     return block_at(x, y, z, c)
 
 
+def aside(k):
+    return (k % 4 == 3) | (k % 8 == 1)
+
+
 def kernel(
-    e_hbm, partner_ref, prior_ref, grad_hbm, lse_ref,
-    own, buf, scores, out, peak, total, lcol, pcol, lnb,
-    load_sem, store_sem, s_up, s_dn, s_far, s_r9, s_r1, s_z, s_loc, s_lse, r_lse, recv,
+    e_hbm, partner_ref, prior_ref, out, lse_ref,
+    own, buf, scores, peak, total, lcol, pcol, lnb, packed,
+    load_sem, s_up, s_dn, s_far, s_r9, s_r1, s_z, s_loc, s_lse, r_lse, recv,
 ):
     b = lax.axis_index("dp") * 8 + lax.axis_index("sub")
     x, y, z, c = coords(b)
@@ -162,13 +166,13 @@
         return copy(held(jnp.where(c == 0, M1, P1), k), mate, jnp.where(c == 0, M9, P9), k, s_loc.at[k])
 
     def z_moves(k):
-        return (rel_z & (k % 2 == 1)) | (z_mid & (k % 4 == 3))
+        return (rel_z & (k % 2 == 1)) | (z_mid & aside(k))
 
     def far_moves(k):
-        return do_far & ~(wrap & (k % 4 == 3))
+        return do_far & ~(wrap & aside(k))
 
     def start_own(k):
-        @pl.when(z_src & (k % 4 == 3))
+        @pl.when(z_src & aside(k))
         def _():
             send_side(k).start()
 
@@ -298,19 +302,22 @@
     summed = jnp.sum(total[...] * jnp.exp2(lane_peak - top), axis=1, keepdims=True)
     both = jnp.maximum(top, prior)
     lse2 = both + jnp.log2(summed * jnp.exp2(top - both) + jnp.exp2(prior - both))
-    lcol[...] = lse2
-    lnb[4] = jnp.transpose(lse2)[0:8, :]
-    lse_ref[...] = lnb[4, 0:1, :] * LN2
+    row = jnp.transpose(lse2)[0:1, :]
+    for i in range(8):
+        packed[4, i : i + 1, :] = row[:, i * 128 : (i + 1) * 128]
 
     def send_lse(t, to):
         return pltpu.make_async_remote_copy(
-            src_ref=lnb.at[4], dst_ref=lnb.at[t], send_sem=s_lse.at[t], recv_sem=r_lse.at[t],
+            src_ref=packed.at[4], dst_ref=packed.at[t], send_sem=s_lse.at[t], recv_sem=r_lse.at[t],
             device_id=device(to), device_id_type=MESH,
         )
 
     lse_sends = [send_lse(M1, near(b, 1)), send_lse(P1, near(b, -1)), send_lse(M9, near(b, 9)), send_lse(P9, near(b, -9))]
     for s in lse_sends:
         s.start()
+    lcol[...] = lse2
+    lnb[4, 0:1, :] = row
+    lse_ref[...] = row * LN2
 
     def weights(t, at):
         parts = []
@@ -325,11 +332,11 @@
     pcol[...] = column(prow)
 
     def own_part(r, carry):
-        at = pl.ds(pl.multiple_of(r * 256, 256), 256)
+        at = pl.ds(pl.multiple_of(r * 512, 512), 512)
         parts = weights(4, at)
         mine = pcol[at, :]
-        row = (lax.broadcasted_iota(jnp.int32, (256, 128), 0) + r * 256).astype(jnp.float32)
-        lane = lax.broadcasted_iota(jnp.int32, (256, 128), 1).astype(jnp.float32)
+        row = (lax.broadcasted_iota(jnp.int32, (512, 128), 0) + r * 512).astype(jnp.float32)
+        lane = lax.broadcasted_iota(jnp.int32, (512, 128), 1).astype(jnp.float32)
         for i in range(8):
             lanes = slice(i * 128, (i + 1) * 128)
             hot = jnp.where(mine == lane + i * 128.0, 1.0, 0.0) + jnp.where(prow[:, lanes] == row, 1.0, 0.0)
@@ -337,25 +344,25 @@
         out[at, :] = jnp.dot(jnp.concatenate(parts, axis=1), own[...], preferred_element_type=jnp.float32)
         return carry
 
-    lax.fori_loop(0, 4, own_part, 0)
-
-    for s in lse_sends:
-        s.wait_recv()
-
-    def rest(r, carry):
-        at = pl.ds(pl.multiple_of(r * 256, 256), 256)
-        acc = out[at, :]
-        for t in (P1, P9, M1, M9):
+    lax.fori_loop(0, 2, own_part, 0)
+
+    order = (P1, M1, P9, M9)
+    for t in order:
+        lse_sends[t].wait_recv()
+        for i in range(8):
+            lnb[t, 0:1, i * 128 : (i + 1) * 128] = packed[t, i : i + 1, :]
+
+        def term(r, carry):
+            at = pl.ds(pl.multiple_of(r * 512, 512), 512)
             w = jnp.concatenate([p.astype(jnp.bfloat16) for p in weights(t, at)], axis=1)
-            term = jnp.dot(w, buf[t], preferred_element_type=jnp.float32)
+            part = jnp.dot(w, buf[t], preferred_element_type=jnp.float32)
             if t in (M1, M9):
-                term = term.astype(jnp.bfloat16).astype(jnp.float32)
-            acc = acc + term
-        out[at, :] = SCALE * acc
-        pltpu.make_async_copy(out.at[at], grad_hbm.at[at], store_sem.at[r]).start()
-        return carry
-
-    lax.fori_loop(0, 4, rest, 0)
+                part = part.astype(jnp.bfloat16).astype(jnp.float32)
+            acc = out[at, :] + part
+            out[at, :] = SCALE * acc if t == order[-1] else acc
+            return carry
+
+        lax.fori_loop(0, ROWS // 512, term, 0)
 
     for s in lse_sends:
         s.wait_send()
@@ -382,7 +389,7 @@
         def _():
             send_r1(k).wait_send()
 
-        @pl.when(z_src & (k % 4 == 3))
+        @pl.when(z_src & aside(k))
         def _():
             send_side(k).wait_send()
 
@@ -393,13 +400,6 @@
         return carry
 
     lax.fori_loop(0, CHUNKS, sent, 0)
-
-    def stored(r, carry):
-        at = pl.ds(pl.multiple_of(r * 256, 256), 256)
-        pltpu.make_async_copy(out.at[at], grad_hbm.at[at], store_sem.at[r]).wait()
-        return carry
-
-    lax.fori_loop(0, 4, stored, 0)
 
 
 def per_device(embeddings, partner, prior_lse):
@@ -409,22 +409,22 @@
         kernel,
         out_shape=(pltpu.VMEM((ROWS, D), f32), jax.ShapeDtypeStruct((1, ROWS), f32)),
         in_specs=[
-            pl.BlockSpec(memory_space=pl.ANY),
+            pl.BlockSpec(memory_space=pltpu.HBM),
             pl.BlockSpec(memory_space=pltpu.VMEM),
             pl.BlockSpec(memory_space=pltpu.VMEM),
         ],
-        out_specs=(pl.BlockSpec(memory_space=pl.ANY), pl.BlockSpec(memory_space=pltpu.VMEM)),
+        out_specs=(pl.BlockSpec(memory_space=pltpu.VMEM), pl.BlockSpec(memory_space=pltpu.VMEM)),
         scratch_shapes=[
             pltpu.VMEM((ROWS, D), jnp.bfloat16),
             pltpu.VMEM((6, ROWS, D), jnp.bfloat16),
             pltpu.VMEM((5, ROWS, ROWS), f32),
-            pltpu.VMEM((ROWS, D), f32),
             pltpu.VMEM((ROWS, 128), f32),
             pltpu.VMEM((ROWS, 128), f32),
             pltpu.VMEM((ROWS, 128), f32),
             pltpu.VMEM((ROWS, 128), f32),
             pltpu.VMEM((5, 8, ROWS), f32),
-            dma, dma((4,)), dma((CHUNKS,)), dma((CHUNKS,)), dma((CHUNKS,)), dma((CHUNKS,)), dma((CHUNKS,)),
+            pltpu.VMEM((5, 8, 128), f32),
+            dma, dma((CHUNKS,)), dma((CHUNKS,)), dma((CHUNKS,)), dma((CHUNKS,)), dma((CHUNKS,)),
             dma((CHUNKS,)), dma((CHUNKS,)), dma((4,)), dma((4,)), dma((6, CHUNKS)),
         ],
         compiler_params=pltpu.CompilerParams(collective_id=0, has_side_effects=True, vmem_limit_bytes=56 << 20),

time: 92.7 us -> 89 us (0.960)
  Pallas kernels: 89.3 us -> 85.6 us
    pallas_call x1, Pallas kernels: 89.3 us -> 85.6 us  [per_device(): pl.pallas_call(kernel, out_shape=(pltpu.VMEM((ROWS, D), f32), jax.ShapeDt...]
where the time goes in v4:
time: 89 us; the launch traced here: 88.9 us
  Pallas kernels  85.6 us (96%)
  local copies, waits for them, and re-layouts  2.61 us (3%)
    pallas_call x1, Pallas kernels, per_device(): pl.pallas_call(kernel, out_shape=(pltpu.VMEM((ROWS, D), f32), jax.ShapeDt...  85.6 us
    unnamed x4, local copies, waits for them, and re-layouts  2.61 us

profile of v4, /device:TPU:1, one launch (start us, length us, event | category | flops | bytes accessed | tf_op | source)
XLA Modules:
  0.0 88.9 jit_solution(3927413080002951608)
XLA Ops:
  0.6 85.6 %shard_map.50 = (f32[1024,1024]{1,0:T(8,128)S(1)}, f32[1,1024]{1,0:T(1,128)}) custom-call(bf16[1024,1024]{1,0:T(8,128)(2,1)} %e_hbm.1, s32[1,1024]{1,0:T(1,128)} %bitcast.4, f32[1,1024]{1,0:T(1,128)} %bitcast.5), custom_call_target="tpu_custom_call" | custom-call | flops 21474836480 | bytes 8388608 | tf_op jit(solution)/shard_map/pallas_call | solution.py:408
  86.3 0.0 copy-start
  86.3 2.0 %copy.7 = f32[1024,1024]{1,0:T(8,128)} copy(f32[1024,1024]{1,0:T(8,128)S(1)} %get-tuple-element.6) | data formatting | bytes 8388608
  88.3 0.0 copy-done
  88.3 0.6 copy.8
Async XLA Ops:
  86.3 2.0 %copy-start = (f32[1,1024]{1,0:T(1,128)S(1)}, f32[1,1024]{1,0:T(1,128)}, u32[]{:S(2)}) copy-start(f32[1,1024]{1,0:T(1,128)} %get-tuple-element.5) | copy-start | bytes 12292

commit v5 on v4

--- a/solution.py
+++ b/solution.py
@@ -57,6 +57,10 @@
     return (k % 4 == 3) | (k % 8 == 1)
 
 
+def by_z(k):
+    return (k % 2 == 1) | (k % 8 == 4)
+
+
 def kernel(
     e_hbm, partner_ref, prior_ref, out, lse_ref,
     own, buf, scores, peak, total, lcol, pcol, lnb, packed,
@@ -130,13 +134,13 @@
         pltpu.make_async_copy(held(slot, k), held(slot, k), recv.at[slot, k]).wait()
 
     def send_up(k):
-        odd = k % 2 == 1
+        odd = by_z(k)
         to = jnp.where(up_sgl & odd, in_column(near(b, 1), 3), up)
         slot = jnp.where(y3, jnp.where(up_sgl & odd, RZ, RL), M1)
         return copy(e_hbm.at[rows(k)], to, slot, k, s_up.at[k])
 
     def send_dn(k):
-        odd = k % 2 == 1
+        odd = by_z(k)
         to = jnp.where(dn_sgl & odd, in_column(near(b, -1), 0), dn)
         slot = jnp.where(y0, jnp.where(dn_sgl & odd, RZ, RL), P1)
         return copy(e_hbm.at[rows(k)], to, slot, k, s_dn.at[k])
@@ -166,7 +170,7 @@
         return copy(held(jnp.where(c == 0, M1, P1), k), mate, jnp.where(c == 0, M9, P9), k, s_loc.at[k])
 
     def z_moves(k):
-        return (rel_z & (k % 2 == 1)) | (z_mid & aside(k))
+        return (rel_z & by_z(k)) | (z_mid & aside(k))
 
     def far_moves(k):
         return do_far & ~(wrap & aside(k))
@@ -216,7 +220,7 @@
 
         @pl.when(k < CHUNKS)
         def _():
-            odd = k % 2 == 1
+            odd = by_z(k)
 
             @pl.when(rel_dbl)
             def _():
@@ -346,6 +350,40 @@
 
     lax.fori_loop(0, 2, own_part, 0)
 
+    def sent(k, carry):
+        odd = by_z(k)
+        @pl.when(k + AHEAD >= CHUNKS)
+        def _():
+            send_up(k).wait_send()
+            send_dn(k).wait_send()
+
+        send_loc(k).wait_send()
+
+        @pl.when(far_moves(k))
+        def _():
+            send_far(k).wait_send()
+
+        @pl.when(rel_dbl)
+        def _():
+            send_r1(k).wait_send()
+            send_r9(k).wait_send()
+
+        @pl.when(rel_sgl & ~odd)
+        def _():
+            send_r1(k).wait_send()
+
+        @pl.when(z_src & aside(k))
+        def _():
+            send_side(k).wait_send()
+
+        @pl.when(z_moves(k))
+        def _():
+            send_z(k).wait_send()
+
+        return carry
+
+    lax.fori_loop(0, CHUNKS, sent, 0)
+
     order = (P1, M1, P9, M9)
     for t in order:
         lse_sends[t].wait_recv()
@@ -362,44 +400,10 @@
             out[at, :] = SCALE * acc if t == order[-1] else acc
             return carry
 
-        lax.fori_loop(0, ROWS // 512, term, 0)
+        lax.fori_loop(0, ROWS // 512, term, 0, unroll=True)
 
     for s in lse_sends:
         s.wait_send()
-
-    def sent(k, carry):
-        odd = k % 2 == 1
-        @pl.when(k + AHEAD >= CHUNKS)
-        def _():
-            send_up(k).wait_send()
-            send_dn(k).wait_send()
-
-        send_loc(k).wait_send()
-
-        @pl.when(far_moves(k))
-        def _():
-            send_far(k).wait_send()
-
-        @pl.when(rel_dbl)
-        def _():
-            send_r1(k).wait_send()
-            send_r9(k).wait_send()
-
-        @pl.when(rel_sgl & ~odd)
-        def _():
-            send_r1(k).wait_send()
-
-        @pl.when(z_src & aside(k))
-        def _():
-            send_side(k).wait_send()
-
-        @pl.when(z_moves(k))
-        def _():
-            send_z(k).wait_send()
-
-        return carry
-
-    lax.fori_loop(0, CHUNKS, sent, 0)
 
 
 def per_device(embeddings, partner, prior_lse):

time: 89 us -> 87.9 us (0.988)
  Pallas kernels: 85.6 us -> 84.5 us
    pallas_call x1, Pallas kernels: 85.6 us -> 84.5 us  [per_device(): pl.pallas_call(kernel, out_shape=(pltpu.VMEM((ROWS, D), f32), jax.ShapeDt...]
where the time goes in v5:
time: 87.9 us; the launch traced here: 87.8 us
  Pallas kernels  84.5 us (96%)
  local copies, waits for them, and re-layouts  2.61 us (3%)
    pallas_call x1, Pallas kernels, per_device(): pl.pallas_call(kernel, out_shape=(pltpu.VMEM((ROWS, D), f32), jax.ShapeDt...  84.5 us
    unnamed x4, local copies, waits for them, and re-layouts  2.61 us

profile of v5, /device:TPU:1, one launch (start us, length us, event | category | flops | bytes accessed | tf_op | source)
XLA Modules:
  0.0 87.8 jit_solution(15016948058563698072)
XLA Ops:
  0.6 84.5 %shard_map.50 = (f32[1024,1024]{1,0:T(8,128)S(1)}, f32[1,1024]{1,0:T(1,128)}) custom-call(bf16[1024,1024]{1,0:T(8,128)(2,1)} %e_hbm.1, s32[1,1024]{1,0:T(1,128)} %bitcast.4, f32[1,1024]{1,0:T(1,128)} %bitcast.5), custom_call_target="tpu_custom_call" | custom-call | flops 21474836480 | bytes 8388608 | tf_op jit(solution)/shard_map/pallas_call | solution.py:412
  85.2 0.0 copy-start
  85.2 2.0 %copy.7 = f32[1024,1024]{1,0:T(8,128)} copy(f32[1024,1024]{1,0:T(8,128)S(1)} %get-tuple-element.6) | data formatting | bytes 8388608
  87.2 0.0 copy-done
  87.2 0.6 copy.8
Async XLA Ops:
  85.2 2.0 %copy-start = (f32[1,1024]{1,0:T(1,128)S(1)}, f32[1,1024]{1,0:T(1,128)}, u32[]{:S(2)}) copy-start(f32[1,1024]{1,0:T(1,128)} %get-tuple-element.5) | copy-start | bytes 12292

commit v6 on v5

--- a/solution.py
+++ b/solution.py
@@ -297,10 +297,11 @@
 
         return carry
 
+    lcol[...] = column(prior_ref[...] * LOG2E)
     load.wait()
     lax.fori_loop(0, CHUNKS + BEHIND, step, 0)
 
-    prior = column(prior_ref[...] * LOG2E)
+    prior = lcol[...]
     lane_peak = peak[...]
     top = jnp.broadcast_to(jnp.max(lane_peak, axis=1, keepdims=True), (ROWS, 128))
     summed = jnp.sum(total[...] * jnp.exp2(lane_peak - top), axis=1, keepdims=True)

time: 87.9 us -> 87.7 us (level)
  no operation moved by 1% of the time
where the time goes in v6:
time: 87.7 us; the launch traced here: 87.6 us
  Pallas kernels  84.3 us (96%)
  local copies, waits for them, and re-layouts  2.61 us (3%)
    pallas_call x1, Pallas kernels, per_device(): pl.pallas_call(kernel, out_shape=(pltpu.VMEM((ROWS, D), f32), jax.ShapeDt...  84.3 us
    unnamed x4, local copies, waits for them, and re-layouts  2.61 us

profile of v6, /device:TPU:1, one launch (start us, length us, event | category | flops | bytes accessed | tf_op | source)
XLA Modules:
  0.0 87.6 jit_solution(11676760509268013199)
XLA Ops:
  0.6 84.3 %shard_map.50 = (f32[1024,1024]{1,0:T(8,128)S(1)}, f32[1,1024]{1,0:T(1,128)}) custom-call(bf16[1024,1024]{1,0:T(8,128)(2,1)} %e_hbm.1, s32[1,1024]{1,0:T(1,128)} %bitcast.4, f32[1,1024]{1,0:T(1,128)} %bitcast.5), custom_call_target="tpu_custom_call" | custom-call | flops 21474836480 | bytes 8388608 | tf_op jit(solution)/shard_map/pallas_call | solution.py:413
  85.0 0.0 copy-start
  85.0 2.0 %copy.7 = f32[1024,1024]{1,0:T(8,128)} copy(f32[1024,1024]{1,0:T(8,128)S(1)} %get-tuple-element.6) | data formatting | bytes 8388608
  87.0 0.0 copy-done
  87.0 0.6 copy.8
Async XLA Ops:
  85.0 2.0 %copy-start = (f32[1,1024]{1,0:T(1,128)S(1)}, f32[1,1024]{1,0:T(1,128)}, u32[]{:S(2)}) copy-start(f32[1,1024]{1,0:T(1,128)} %get-tuple-element.5) | copy-start | bytes 12292
